TPU v7x, 256 devices: a whole 4x4x8 slice. The times are simulated.
256 devices in a mesh: row: 32 (over z, x), col: 8 (over y, core).
Axes of the slice: x: 4, y: 4, z: 8, core: 2. Of those that a mesh axis runs over, the one named last changes fastest.
Arguments:
- src_points: float32 [3, 8192], P(None, 'row'), may hold values from 0 to 3
- tgt_points: float32 [3, 262144], P(None, 'col'), may hold values from 0 to 1
- src_mass: float32 [8192], P('row'), may hold values from 1 to 90
- tgt_mass: float32 [262144], P('col'), may hold values from 1 to 90
Outputs:
- src_pot: float32 [8192], P('row')
- tgt_pot: float32 [262144], P('col')
All inputs are finite; a program needn't handle non-finite values.
Results may differ from a plain program's by a relative error of at most 0.0003.
Values sent between devices are 32-bit elements; how exact they have to be, the bound alone decides.
No kernel may reach another device: no remote copies, remote signals or barrier semaphores. Data moves between devices by JAX's collectives and lax.ppermute only.
A program may use at most 64 MiB of HBM per device.

v0:
```python
import functools
import math

import jax
import jax.numpy as jnp
from jax import lax
from jax.experimental import pallas as pl
from jax.experimental.pallas import tpu as pltpu
from jax.sharding import Mesh, PartitionSpec as P

EPSILON = 0.01
LN2 = math.log(2.0)
SCALE = 1.0 / (EPSILON * LN2)
CENTER = 0.5
FLOOR1 = 2.0**-60
FLOOR2 = 2.0**-40
BF16 = jnp.bfloat16
F32 = jnp.float32

Z, X, Y, C = 8, 4, 4, 2
NCOL = Y * C
GROUP = X * NCOL


def pieces(v):
    p1 = v.astype(BF16).astype(F32)
    r = v - p1
    p2 = r.astype(BF16).astype(F32)
    p3 = (r - p2).astype(BF16).astype(F32)
    return p1, p2, p3


def stack_src(v):
    p1, p2, p3 = pieces(v)
    return [
        jnp.concatenate([p1, p2], axis=0),
        jnp.concatenate([p3, p1], axis=0),
        jnp.concatenate([p2, p1], axis=0),
    ]


def stack_tgt(v):
    p1, p2, p3 = pieces(v)
    return [
        jnp.concatenate([p1, p1], axis=0),
        jnp.concatenate([p1, p2], axis=0),
        jnp.concatenate([p2, p3], axis=0),
    ]


def scores(lhs, rhs):
    return lax.dot_general(
        lhs, rhs, (((1,), (0,)), ((), ())), preferred_element_type=F32
    )


def fold(v, op):
    out = v[:, 0:128]
    for k in range(128, v.shape[1], 128):
        out = op(out, v[:, k : k + 128])
    return out


def src_side(x_ref, use_mass):
    n = x_ref.shape[1]
    x_ref[0:3, :] = x_ref[0:3, :] - CENTER
    a, b, c = x_ref[0:1, :], x_ref[1:2, :], x_ref[2:3, :]
    x_ref[3:4, :] = x_ref[3:4, :] - SCALE * (a * a + b * b + c * c)
    x_ref[0:3, :] = x_ref[0:3, :] * (2.0 * SCALE)
    x_ref[4:7, :] = jnp.ones((3, n), F32)
    x_ref[7:8, :] = jnp.full((1, n), use_mass, F32)
    stacked = jnp.concatenate(stack_src(x_ref[...]), axis=0)
    return jnp.transpose(stacked).astype(BF16)


def row_of(tile):
    return jnp.concatenate([tile[s : s + 1, :] for s in range(tile.shape[0])], axis=1)


def set_tile(ref, row):
    for s in range(row.shape[1] // 128):
        ref[s : s + 1, :] = row[:, 128 * s : 128 * s + 128]


def row_kernel(
    src_hbm,
    src_mass_hbm,
    tgt_hbm,
    mass_hbm,
    out_ref,
    share_ref,
    log_ref,
    src_ref,
    src_mass_ref,
    tgt_ref,
    mass_ref,
    sem,
    x_ref,
    t_ref,
    w_ref,
    o_ref,
):
    n = tgt_ref.shape[1]
    rows = src_ref.shape[1]
    parts = [slice(0, n // 8), slice(n // 8, n)]
    pairs = [(src_hbm, src_ref), (src_mass_hbm, src_mass_ref)]
    for lanes in parts:
        pairs.append((tgt_hbm.at[:, lanes], tgt_ref.at[:, lanes]))
        pairs.append((mass_hbm.at[:, lanes], mass_ref.at[:, lanes]))
    moves = [pltpu.make_async_copy(a, b, sem.at[i]) for i, (a, b) in enumerate(pairs)]
    for move in moves:
        move.start()
    moves[0].wait()
    x_ref[0:3, :] = src_ref[...]
    x_ref[3:4, :] = jnp.zeros((1, rows), F32)
    lhs = src_side(x_ref, 1.0)
    moves[1].wait()
    acc = jnp.zeros((rows, 128), F32)
    for k, lanes in enumerate(parts):
        moves[2 * k + 2].wait()
        moves[2 * k + 3].wait()
        points = tgt_ref[:, lanes] - CENTER
        t_ref[0:3, lanes] = points
        t_ref[3:4, lanes] = jnp.ones((1, points.shape[1]), F32)
        t_ref[4:7, lanes] = points * points * -SCALE
        t_ref[7:8, lanes] = jnp.log2(mass_ref[:, lanes])
        for i, part in enumerate(stack_tgt(t_ref[:, lanes])):
            w_ref[16 * i : 16 * i + 16, lanes] = part.astype(BF16)
        acc = acc + fold(jnp.exp2(scores(lhs, w_ref[:, lanes])), jnp.add)
    total = jnp.sum(jnp.transpose(acc), axis=0, keepdims=True)
    set_tile(o_ref, jnp.log2(total))

    @pl.when(jnp.min(total) < FLOOR1)
    def _():
        small = 1024

        def block(k):
            return scores(lhs, w_ref[:, pl.ds(pl.multiple_of(k * small, small), small)])

        def top(k, m):
            return jnp.maximum(m, fold(block(k), jnp.maximum))

        m = lax.fori_loop(0, n // small, top, jnp.full((rows, 128), -jnp.inf, F32))
        m = jnp.max(m, axis=1, keepdims=True)

        def shifted(k, acc):
            return acc + fold(jnp.exp2(block(k) - m), jnp.add)

        acc = lax.fori_loop(0, n // small, shifted, jnp.zeros((rows, 128), F32))
        total = jnp.sum(jnp.transpose(acc), axis=0, keepdims=True)
        peak = jnp.transpose(jnp.broadcast_to(m, (rows, 128)))[0:1, :]
        set_tile(o_ref, jnp.log2(total) + peak)

    col = lax.axis_index("y") * C + lax.axis_index("c")
    info = src_mass_ref[...]
    for d in range(3):
        info = jnp.where(col == d, src_ref[d : d + 1, :], info)
    for s in range(rows // 128):
        o_ref[2 + s : 3 + s, :] = info[:, 128 * s : 128 * s + 128]
    for p in range(out_ref.shape[0]):
        out_ref[p] = o_ref[...]
    share = share_ref.shape[1]
    mine = pl.ds(pl.multiple_of(lax.axis_index("x") * share, share), share)
    share_ref[...] = w_ref[:, mine]
    log_ref[...] = t_ref[7:8, mine]


def set_src(first_ref, x_ref):
    logs, masses = [], []
    for x in range(X):
        parts = [first_ref[x * NCOL + q] for q in range(NCOL)]
        peak = functools.reduce(jnp.maximum, parts)
        total = functools.reduce(jnp.add, [jnp.exp2(v - peak) for v in parts])
        log_sum = peak + jnp.log2(total)
        for s in range(2):
            lanes = slice(256 * x + 128 * s, 256 * x + 128 * s + 128)
            for d in range(3):
                x_ref[d : d + 1, lanes] = parts[d][2 + s : 3 + s, :]
            logs.append(log_sum[s : s + 1, :])
            masses.append(parts[3][2 + s : 3 + s, :])
    mass = jnp.concatenate(masses, axis=1)
    return jnp.log2(mass), mass, jnp.concatenate(logs, axis=1)


def col_kernel(
    first_ref, w_ref, qa_ref, qb_ref, out_ref, shift_ref, src_ref, x_ref, s_ref
):
    chunk = s_ref.shape[1]
    log_mass, mass, log_sum = set_src(first_ref, x_ref)
    src_ref[...] = jnp.zeros(src_ref.shape, F32)
    src_ref[0:1, :] = log_mass - log_sum
    src_ref[1:2, :] = mass
    x_ref[3:4, :] = log_mass - log_sum
    lhs = src_side(x_ref, 0.0)

    def block(k):
        return scores(lhs, w_ref[:, pl.ds(pl.multiple_of(k * chunk, chunk), chunk)])

    for half, q_ref in enumerate((qa_ref, qb_ref)):

        def step(k, carry, half=half, q_ref=q_ref):
            q = jnp.exp2(block(4 * half + k))
            q_ref[:, pl.ds(pl.multiple_of(k * chunk, chunk), chunk)] = q
            s_ref[pl.ds(4 * half + k, 1), :] = jnp.sum(q, axis=0, keepdims=True)
            return carry

        lax.fori_loop(0, 4, step, 0, unroll=4)
    total = s_ref[...]
    s_ref[...] = jnp.log2(total)
    shift_ref[...] = jnp.zeros(shift_ref.shape, F32)

    @pl.when(jnp.min(total) < FLOOR2)
    def _():
        for half, q_ref in enumerate((qa_ref, qb_ref)):

            def shifted(k, carry, half=half, q_ref=q_ref):
                s = block(4 * half + k)
                m = jnp.max(s, axis=0, keepdims=True)
                q = jnp.exp2(s - m)
                q_ref[:, pl.ds(pl.multiple_of(k * chunk, chunk), chunk)] = q
                l = jnp.sum(q, axis=0, keepdims=True)
                s_ref[pl.ds(4 * half + k, 1), :] = m + jnp.log2(l)
                shift_ref[pl.ds(4 * half + k, 1), :] = m
                return carry

            lax.fori_loop(0, 4, shifted, 0)

    for p in range(Z):
        out_ref[p] = s_ref[...]


def mid_kernel(
    cols_ref, qa_ref, qb_ref, shift_ref, mass_ref, out_ref, scale_ref, log_ref, acc_ref, o_ref
):
    chunk = log_ref.shape[1]
    parts = [cols_ref[z] for z in range(Z)]
    peak = functools.reduce(jnp.maximum, parts)
    total = functools.reduce(jnp.add, [jnp.exp2(v - peak) for v in parts])
    log_col = peak + jnp.log2(total)
    log_ref[...] = log_col
    scale_ref[...] = shift_ref[...] - log_col
    acc_ref[...] = jnp.zeros(acc_ref.shape, F32)

    for half, q_ref in enumerate((qa_ref, qb_ref)):

        def step(k, carry, half=half, q_ref=q_ref):
            weights = []
            for e in range(2):
                row = 4 * half + 2 * k + e
                log_mass = mass_ref[:, pl.ds(pl.multiple_of(row * chunk, chunk), chunk)]
                w = jnp.exp2(log_mass + scale_ref[pl.ds(row, 1), :])
                for j in range(0, chunk, 128):
                    weights.append(jnp.broadcast_to(w[:, j : j + 128], (8, 128)))
            cols = pl.ds(pl.multiple_of(2 * k * chunk, 2 * chunk), 2 * chunk)
            for h in range(0, acc_ref.shape[0], 8):
                q = q_ref[h : h + 8, cols]
                terms = [q[:, 128 * j : 128 * j + 128] * w for j, w in enumerate(weights)]
                while len(terms) > 1:
                    terms = [u + v for u, v in zip(terms[::2], terms[1::2])]
                acc_ref[h : h + 8, :] += terms[0]
            return carry

        lax.fori_loop(0, 2, step, 0)
    scale_ref[...] = jnp.exp2(scale_ref[...])
    set_tile(o_ref, jnp.sum(jnp.transpose(acc_ref[...]), axis=0, keepdims=True))
    for p in range(out_ref.shape[0]):
        out_ref[p] = o_ref[...]


def last_kernel(ratio_ref, qa_ref, qb_ref, src_ref, scale_ref, out_ref, pot_ref, r_ref, s_ref):
    chunk = s_ref.shape[1]
    ratio = ratio_ref[0]
    for p in range(1, ratio_ref.shape[0]):
        ratio = ratio + ratio_ref[p]
    ratio = row_of(ratio)
    mass = src_ref[1:2, :]
    r_ref[...] = jnp.transpose(jnp.broadcast_to(mass / ratio, (128, ratio.shape[1])))
    s_ref[0:1, :] = LN2 * (src_ref[0:1, :] - jnp.log2(ratio))
    rows = pot_ref.shape[1]
    mine = pl.multiple_of(lax.axis_index("x") * rows, rows)
    pot_ref[...] = s_ref[0:1, pl.ds(mine, rows)]
    for half, q_ref in enumerate((qa_ref, qb_ref)):

        def step(k, carry, half=half, q_ref=q_ref):
            cols = pl.ds(pl.multiple_of(k * chunk, chunk), chunk)
            accs = [jnp.zeros((8, 128), F32)] * (chunk // 128)
            for h in range(0, r_ref.shape[0], 8):
                r = r_ref[h : h + 8, :]
                q = q_ref[h : h + 8, cols]
                for j in range(chunk // 128):
                    accs[j] = accs[j] + q[:, 128 * j : 128 * j + 128] * r
            acc = jnp.concatenate(accs, axis=1)
            s_ref[pl.ds(4 * half + k, 1), :] = jnp.sum(acc, axis=0, keepdims=True)
            return carry

        lax.fori_loop(0, 4, step, 0)
    lane = lax.broadcasted_iota(jnp.int32, (1, 128), 1)
    extra = jnp.where(lane == 0, jnp.sum(mass), jnp.sum(ratio))
    s_ref[...] = s_ref[...] * scale_ref[...]
    for k in range(8):
        row = s_ref[k : k + 1, :]
        for p in range(Z):
            out_ref[p, :, k * chunk : (k + 1) * chunk] = row
    for p in range(Z):
        out_ref[p, :, 8 * chunk : 8 * chunk + 128] = extra


def end_kernel(cols_ref, log_ref, pot_ref, out_ref, src_hbm, src_ref, sem, o_ref, s_ref):
    chunk = log_ref.shape[1]
    def over_z(lanes):
        return functools.reduce(jnp.add, [cols_ref[z, :, lanes] for z in range(Z)])

    sums = jnp.log(over_z(slice(8 * chunk, 8 * chunk + 128)))
    log_src, log_tgt = sums[:, 0:1], sums[:, 1:2]
    src_ref[...] = pot_ref[...] + (2.0 * log_tgt - log_src)
    move = pltpu.make_async_copy(src_ref, src_hbm, sem)
    move.start()
    for k in range(8):
        s_ref[k : k + 1, :] = over_z(slice(k * chunk, (k + 1) * chunk))
    total = s_ref[...]
    pot = -LN2 * (jnp.log2(total) + log_ref[...]) + 2.0 * (log_src - log_tgt)
    per = chunk // 128
    for k in range(8):
        for s in range(per):
            o_ref[per * k + s : per * k + s + 1, :] = pot[k : k + 1, 128 * s : 128 * s + 128]
    for p in range(X):
        out_ref[p] = o_ref[...]
    move.wait()


def kernel_call(body, out_shape, scratch, args, space=pltpu.VMEM, megabytes=8):
    vmem = pl.BlockSpec(memory_space=pltpu.VMEM)
    return pl.pallas_call(
        body,
        out_shape=[
            jax.ShapeDtypeStruct(s, F32) if isinstance(s, tuple) else s for s in out_shape
        ],
        in_specs=[pl.BlockSpec(memory_space=space)] * len(args),
        out_specs=[vmem] * len(out_shape),
        scratch_shapes=scratch,
        compiler_params=pltpu.CompilerParams(vmem_limit_bytes=megabytes * 2**20),
    )(*args)


def trade(v, axes):
    return lax.all_to_all(v, axes, 0, 0)


def on_device(src_points, tgt_points, src_mass, tgt_mass):
    rows = src_points.shape[1]
    cols = tgt_points.shape[1]
    nsrc = rows * X
    ntgt = cols // X
    chunk = ntgt // 8

    first, share, log_mass = kernel_call(
        row_kernel,
        [(GROUP, 4, 128), jax.ShapeDtypeStruct((48, ntgt), BF16), (1, ntgt)],
        [
            pltpu.VMEM((3, rows), F32),
            pltpu.VMEM((1, rows), F32),
            pltpu.VMEM((3, cols), F32),
            pltpu.VMEM((1, cols), F32),
            pltpu.SemaphoreType.DMA((6,)),
            pltpu.VMEM((8, rows), F32),
            pltpu.VMEM((8, cols), F32),
            pltpu.VMEM((48, cols), BF16),
            pltpu.VMEM((4, 128), F32),
        ],
        [
            pltpu.with_memory_space_constraint(v, pltpu.HBM)
            for v in (src_points, src_mass.reshape(1, rows), tgt_points, tgt_mass.reshape(1, cols))
        ],
        space=pltpu.HBM,
        megabytes=50,
    )
    first = trade(first, ("x", "y", "c"))
    half = pltpu.VMEM((nsrc, ntgt // 2), F32)
    *q, logs, shift, src_rows = kernel_call(
        col_kernel,
        [half, half, (Z, 8, chunk), (8, chunk), (8, nsrc)],
        [
            pltpu.VMEM((8, nsrc), F32),
            pltpu.VMEM((8, chunk), F32),
        ],
        (first, share),
    )
    q = [pltpu.with_memory_space_constraint(v, pltpu.VMEM) for v in q]
    logs = trade(logs, "z")
    ratio, scale, log_col = kernel_call(
        mid_kernel,
        [(GROUP, 8, 128), (8, chunk), (8, chunk)],
        [pltpu.VMEM((nsrc, 128), F32), pltpu.VMEM((8, 128), F32)],
        (logs, *q, shift, log_mass),
        megabytes=4,
    )
    ratio = trade(ratio, ("x", "y", "c"))
    col_sums, pot = kernel_call(
        last_kernel,
        [(Z, 1, ntgt + 128), (1, rows)],
        [pltpu.VMEM((nsrc, 128), F32), pltpu.VMEM((8, chunk), F32)],
        (ratio, *q, src_rows, scale),
        megabytes=4,
    )
    col_sums = trade(col_sums, "z")
    vmem = pl.BlockSpec(memory_space=pltpu.VMEM)
    tgt_pot, src_pot = pl.pallas_call(
        end_kernel,
        out_shape=[
            jax.ShapeDtypeStruct((X, ntgt // 128, 128), F32),
            pltpu.HBM((1, rows), F32),
        ],
        in_specs=[vmem] * 3,
        out_specs=[vmem, pl.BlockSpec(memory_space=pltpu.HBM)],
        scratch_shapes=[
            pltpu.VMEM((1, rows), F32),
            pltpu.SemaphoreType.DMA,
            pltpu.VMEM((ntgt // 128, 128), F32),
            pltpu.VMEM((8, chunk), F32),
        ],
        compiler_params=pltpu.CompilerParams(vmem_limit_bytes=4 * 2**20),
    )(col_sums, log_col, pot)
    return (src_pot.reshape(rows), trade(tgt_pot, "x").reshape(cols))


def solution(mesh):
    fine = Mesh(mesh.devices.reshape(Z, X, Y, C), ("z", "x", "y", "c"))
    row, col = ("z", "x"), ("y", "c")
    placed = (P(None, row), P(None, col), P(row), P(col))
    return jax.shard_map(
        on_device, mesh=fine, in_specs=placed, out_specs=(P(row), P(col)), check_vma=False
    )
```

profile of v0, /device:TPU:1, one launch (start us, length us, event | category | flops | bytes accessed | tf_op | source)
XLA Modules:
  0.0 116.7 jit_solution(9601507924496316517)
XLA Ops:
  0.6 24.4 %shard_map.59 = (f32[32,4,128]{2,1,0:T(4,128)S(1)}, bf16[48,8192]{1,0:T(8,128)(2,1)S(1)}, f32[1,8192]{1,0:T(1,128)S(1)}) custom-call(f32[3,256]{1,0:T(4,128)} %src_hbm.1, f32[1,256]{1,0:T(1,128)} %bitcast.6, f32[3,32768]{1,0:T(4,128)} %tgt_hbm.1, f32[1,32768]{1,0:T(1,128)} %bitcast.5), custom_call_target="tpu_custom_call" | custom-call | tf_op jit(solution)/shard_map/pallas_call | solution.py:333
  25.1 15.7 %all_to_all.25.first_ref = f32[32,4,128]{2,1,0:T(4,128)S(1)} all-to-all(f32[32,4,128]{2,1,0:T(4,128)S(1)} %get-tuple-element.17), channel_id=1, replica_groups=mesh['z'=8,'x'=4,'y'=4,'c'=2] {'x','y','c'}, dimensions={0} | all-to-all | bytes 131072 | tf_op jit(solution)/shard_map/all_to_all | solution.py:346
  40.8 15.7 %shard_map.60 = (f32[1024,4096]{1,0:T(8,128)S(1)}, f32[1024,4096]{1,0:T(8,128)S(1)}, f32[8,8,1024]{2,1,0:T(8,128)S(1)}, f32[8,1024]{1,0:T(8,128)S(1)}, f32[8,1024]{1,0:T(8,128)S(1)}) custom-call(f32[32,4,128]{2,1,0:T(4,128)S(1)} %all_to_all.25.first_ref, bf16[48,8192]{1,0:T(8,128)(2,1)S(1)} %get-tuple-element.18.w_ref), custom_call_target="tpu_custom_call" | custom-call | tf_op jit(solution)/shard_map/pallas_call | solution.py:333
  56.6 19.0 %all_to_all.26.cols_ref = f32[8,8,1024]{2,1,0:T(8,128)S(1)} all-to-all(f32[8,8,1024]{2,1,0:T(8,128)S(1)} %get-tuple-element.19), channel_id=1, replica_groups=mesh['z'=8,'x'=4,'y'=4,'c'=2] {'z'}, dimensions={0} | all-to-all | bytes 524288 | tf_op jit(solution)/shard_map/all_to_all | solution.py:346
  75.5 2.5 %shard_map.61 = (f32[32,8,128]{2,1,0:T(8,128)S(1)}, f32[8,1024]{1,0:T(8,128)S(1)}, f32[8,1024]{1,0:T(8,128)S(1)}) custom-call(f32[8,8,1024]{2,1,0:T(8,128)S(1)} %all_to_all.26.cols_ref, f32[1024,4096]{1,0:T(8,128)S(1)} %get-tuple-element.20.qa_ref, f32[1024,4096]{1,0:T(8,128)S(1)} %get-tuple-element.21.qb_ref, f32[8,1024]{1,0:T(8,128)S(1)} %get-tuple-element.22.shift_ref, ...), custom_call_target="tpu_custom_call" | custom-call | tf_op jit(solution)/shard_map/pallas_call | solution.py:333
  78.1 12.5 %all_to_all.27.ratio_ref = f32[32,8,128]{2,1,0:T(8,128)S(1)} all-to-all(f32[32,8,128]{2,1,0:T(8,128)S(1)} %get-tuple-element.24), channel_id=1, replica_groups=mesh['z'=8,'x'=4,'y'=4,'c'=2] {'x','y','c'}, dimensions={0} | all-to-all | bytes 262144 | tf_op jit(solution)/shard_map/all_to_all | solution.py:346
  90.6 2.6 %shard_map.62 = (f32[8,1,8320]{2,1,0:T(1,128)S(1)}, f32[1,256]{1,0:T(1,128)S(1)}) custom-call(f32[32,8,128]{2,1,0:T(8,128)S(1)} %all_to_all.27.ratio_ref, f32[1024,4096]{1,0:T(8,128)S(1)} %get-tuple-element.20.qa_ref, f32[1024,4096]{1,0:T(8,128)S(1)} %get-tuple-element.21.qb_ref, f32[8,1024]{1,0:T(8,128)S(1)} %get-tuple-element.25.src_ref, ...), custom_call_target="tpu_custom_call" | custom-call | tf_op jit(solution)/shard_map/pallas_call | solution.py:333
  93.3 14.8 %all_to_all.28.cols_ref = f32[8,1,8320]{2,1,0:T(1,128)S(1)} all-to-all(f32[8,1,8320]{2,1,0:T(1,128)S(1)} %get-tuple-element.27), channel_id=1, replica_groups=mesh['z'=8,'x'=4,'y'=4,'c'=2] {'z'}, dimensions={0} | all-to-all | bytes 532480 | tf_op jit(solution)/shard_map/all_to_all | solution.py:346
  108.0 0.7 shard_map.63
  108.8 7.2 %all_to_all.29 = f32[4,64,128]{2,1,0:T(8,128)S(1)} all-to-all(f32[4,64,128]{2,1,0:T(8,128)S(1)} %get-tuple-element.31), channel_id=1, replica_groups=mesh['z'=8,'x'=4,'y'=4,'c'=2] {'x'}, dimensions={0} | all-to-all | bytes 262144 | tf_op jit(solution)/shard_map/all_to_all | solution.py:346
  116.0 0.7 copy.7
where the time goes:
time: 117 us
  blocking collectives  69.3 us (59%)
  Pallas kernels  46.1 us (39%)
    all_to_all x5, blocking collectives, trade(): return lax.all_to_all(v, axes, 0, 0)  69.3 us
    pallas_call x4, Pallas kernels, kernel_call(): pl.pallas_call(body, out_shape=[jax.ShapeDtypeStruct(s, F32) if isinstanc...  45.3 us

commit v1 on v0

--- a/solution.py
+++ b/solution.py
@@ -88,7 +88,7 @@
     tgt_hbm,
     mass_hbm,
     out_ref,
-    share_ref,
+    w_ref,
     log_ref,
     src_ref,
     src_mass_ref,
@@ -97,7 +97,6 @@
     sem,
     x_ref,
     t_ref,
-    w_ref,
     o_ref,
 ):
     n = tgt_ref.shape[1]
@@ -159,10 +158,8 @@
         o_ref[2 + s : 3 + s, :] = info[:, 128 * s : 128 * s + 128]
     for p in range(out_ref.shape[0]):
         out_ref[p] = o_ref[...]
-    share = share_ref.shape[1]
-    mine = pl.ds(pl.multiple_of(lax.axis_index("x") * share, share), share)
-    share_ref[...] = w_ref[:, mine]
-    log_ref[...] = t_ref[7:8, mine]
+    share = log_ref.shape[1]
+    log_ref[...] = t_ref[7:8, pl.ds(pl.multiple_of(lax.axis_index("x") * share, share), share)]
 
 
 def set_src(first_ref, x_ref):
@@ -193,8 +190,10 @@
     x_ref[3:4, :] = log_mass - log_sum
     lhs = src_side(x_ref, 0.0)
 
+    begin = lax.axis_index("x") * (8 * chunk)
+
     def block(k):
-        return scores(lhs, w_ref[:, pl.ds(pl.multiple_of(k * chunk, chunk), chunk)])
+        return scores(lhs, w_ref[:, pl.ds(pl.multiple_of(begin + k * chunk, chunk), chunk)])
 
     for half, q_ref in enumerate((qa_ref, qb_ref)):
 
@@ -353,9 +352,9 @@
     ntgt = cols // X
     chunk = ntgt // 8
 
-    first, share, log_mass = kernel_call(
+    first, pieces_all, log_mass = kernel_call(
         row_kernel,
-        [(GROUP, 4, 128), jax.ShapeDtypeStruct((48, ntgt), BF16), (1, ntgt)],
+        [(GROUP, 4, 128), pltpu.VMEM((48, cols), BF16), (1, ntgt)],
         [
             pltpu.VMEM((3, rows), F32),
             pltpu.VMEM((1, rows), F32),
@@ -364,7 +363,6 @@
             pltpu.SemaphoreType.DMA((6,)),
             pltpu.VMEM((8, rows), F32),
             pltpu.VMEM((8, cols), F32),
-            pltpu.VMEM((48, cols), BF16),
             pltpu.VMEM((4, 128), F32),
         ],
         [
@@ -383,7 +381,7 @@
             pltpu.VMEM((8, nsrc), F32),
             pltpu.VMEM((8, chunk), F32),
         ],
-        (first, share),
+        (first, pltpu.with_memory_space_constraint(pieces_all, pltpu.VMEM)),
     )
     q = [pltpu.with_memory_space_constraint(v, pltpu.VMEM) for v in q]
     logs = trade(logs, "z")

time: 117 us -> 117 us (level)
  no operation moved by 1% of the time
where the time goes in v1:
time: 117 us; the launch traced here: 116 us
  blocking collectives  69.3 us (59%)
  Pallas kernels  45.7 us (39%)
    all_to_all x5, blocking collectives, trade(): return lax.all_to_all(v, axes, 0, 0)  69.3 us
    pallas_call x4, Pallas kernels, kernel_call(): pl.pallas_call(body, out_shape=[jax.ShapeDtypeStruct(s, F32) if isinstanc...  45 us

profile of v1, /device:TPU:1, one launch (start us, length us, event | category | flops | bytes accessed | tf_op | source)
XLA Modules:
  0.0 116.4 jit_solution(12084367696261976833)
XLA Ops:
  0.6 24.2 %shard_map.59 = (f32[32,4,128]{2,1,0:T(4,128)S(1)}, bf16[48,32768]{1,0:T(8,128)(2,1)S(1)}, f32[1,8192]{1,0:T(1,128)S(1)}) custom-call(f32[3,256]{1,0:T(4,128)} %src_hbm.1, f32[1,256]{1,0:T(1,128)} %bitcast.6, f32[3,32768]{1,0:T(4,128)} %tgt_hbm.1, f32[1,32768]{1,0:T(1,128)} %bitcast.5), custom_call_target="tpu_custom_call" | custom-call | tf_op jit(solution)/shard_map/pallas_call | solution.py:332
  24.8 15.8 %all_to_all.25.first_ref = f32[32,4,128]{2,1,0:T(4,128)S(1)} all-to-all(f32[32,4,128]{2,1,0:T(4,128)S(1)} %get-tuple-element.17), channel_id=1, replica_groups=mesh['z'=8,'x'=4,'y'=4,'c'=2] {'x','y','c'}, dimensions={0} | all-to-all | bytes 131072 | tf_op jit(solution)/shard_map/all_to_all | solution.py:345
  40.6 15.7 %shard_map.60 = (f32[1024,4096]{1,0:T(8,128)S(1)}, f32[1024,4096]{1,0:T(8,128)S(1)}, f32[8,8,1024]{2,1,0:T(8,128)S(1)}, f32[8,1024]{1,0:T(8,128)S(1)}, f32[8,1024]{1,0:T(8,128)S(1)}) custom-call(f32[32,4,128]{2,1,0:T(4,128)S(1)} %all_to_all.25.first_ref, bf16[48,32768]{1,0:T(8,128)(2,1)S(1)} %get-tuple-element.18.w_ref), custom_call_target="tpu_custom_call" | custom-call | tf_op jit(solution)/shard_map/pallas_call | solution.py:332
  56.2 19.0 %all_to_all.26.cols_ref = f32[8,8,1024]{2,1,0:T(8,128)S(1)} all-to-all(f32[8,8,1024]{2,1,0:T(8,128)S(1)} %get-tuple-element.19), channel_id=1, replica_groups=mesh['z'=8,'x'=4,'y'=4,'c'=2] {'z'}, dimensions={0} | all-to-all | bytes 524288 | tf_op jit(solution)/shard_map/all_to_all | solution.py:345
  75.3 2.5 %shard_map.61 = (f32[32,8,128]{2,1,0:T(8,128)S(1)}, f32[8,1024]{1,0:T(8,128)S(1)}, f32[8,1024]{1,0:T(8,128)S(1)}) custom-call(f32[8,8,1024]{2,1,0:T(8,128)S(1)} %all_to_all.26.cols_ref, f32[1024,4096]{1,0:T(8,128)S(1)} %get-tuple-element.20.qa_ref, f32[1024,4096]{1,0:T(8,128)S(1)} %get-tuple-element.21.qb_ref, f32[8,1024]{1,0:T(8,128)S(1)} %get-tuple-element.22.shift_ref, ...), custom_call_target="tpu_custom_call" | custom-call | tf_op jit(solution)/shard_map/pallas_call | solution.py:332
  77.8 12.5 %all_to_all.27.ratio_ref = f32[32,8,128]{2,1,0:T(8,128)S(1)} all-to-all(f32[32,8,128]{2,1,0:T(8,128)S(1)} %get-tuple-element.24), channel_id=1, replica_groups=mesh['z'=8,'x'=4,'y'=4,'c'=2] {'x','y','c'}, dimensions={0} | all-to-all | bytes 262144 | tf_op jit(solution)/shard_map/all_to_all | solution.py:345
  90.3 2.6 %shard_map.62 = (f32[8,1,8320]{2,1,0:T(1,128)S(1)}, f32[1,256]{1,0:T(1,128)S(1)}) custom-call(f32[32,8,128]{2,1,0:T(8,128)S(1)} %all_to_all.27.ratio_ref, f32[1024,4096]{1,0:T(8,128)S(1)} %get-tuple-element.20.qa_ref, f32[1024,4096]{1,0:T(8,128)S(1)} %get-tuple-element.21.qb_ref, f32[8,1024]{1,0:T(8,128)S(1)} %get-tuple-element.25.src_ref, ...), custom_call_target="tpu_custom_call" | custom-call | tf_op jit(solution)/shard_map/pallas_call | solution.py:332
  93.0 14.8 %all_to_all.28.cols_ref = f32[8,1,8320]{2,1,0:T(1,128)S(1)} all-to-all(f32[8,1,8320]{2,1,0:T(1,128)S(1)} %get-tuple-element.27), channel_id=1, replica_groups=mesh['z'=8,'x'=4,'y'=4,'c'=2] {'z'}, dimensions={0} | all-to-all | bytes 532480 | tf_op jit(solution)/shard_map/all_to_all | solution.py:345
  107.8 0.7 shard_map.63
  108.5 7.2 %all_to_all.29 = f32[4,64,128]{2,1,0:T(8,128)S(1)} all-to-all(f32[4,64,128]{2,1,0:T(8,128)S(1)} %get-tuple-element.31), channel_id=1, replica_groups=mesh['z'=8,'x'=4,'y'=4,'c'=2] {'x'}, dimensions={0} | all-to-all | bytes 262144 | tf_op jit(solution)/shard_map/all_to_all | solution.py:345
  115.7 0.7 copy.7

commit v2 on v1

--- a/solution.py
+++ b/solution.py
@@ -107,8 +107,8 @@
         pairs.append((tgt_hbm.at[:, lanes], tgt_ref.at[:, lanes]))
         pairs.append((mass_hbm.at[:, lanes], mass_ref.at[:, lanes]))
     moves = [pltpu.make_async_copy(a, b, sem.at[i]) for i, (a, b) in enumerate(pairs)]
-    for move in moves:
-        move.start()
+    for i in (2, 3, 0, 4, 5, 1):
+        moves[i].start()
     moves[0].wait()
     x_ref[0:3, :] = src_ref[...]
     x_ref[3:4, :] = jnp.zeros((1, rows), F32)

time: 117 us -> 117 us (level)
  no operation moved by 1% of the time
where the time goes in v2:
time: 117 us; the launch traced here: 116 us
  blocking collectives  69.3 us (59%)
  Pallas kernels  45.8 us (39%)
    all_to_all x5, blocking collectives, trade(): return lax.all_to_all(v, axes, 0, 0)  69.3 us
    pallas_call x4, Pallas kernels, kernel_call(): pl.pallas_call(body, out_shape=[jax.ShapeDtypeStruct(s, F32) if isinstanc...  45.1 us

profile of v2, /device:TPU:1, one launch (start us, length us, event | category | flops | bytes accessed | tf_op | source)
XLA Modules:
  0.0 116.4 jit_solution(15848290670248722200)
XLA Ops:
  0.6 24.2 %shard_map.59 = (f32[32,4,128]{2,1,0:T(4,128)S(1)}, bf16[48,32768]{1,0:T(8,128)(2,1)S(1)}, f32[1,8192]{1,0:T(1,128)S(1)}) custom-call(f32[3,256]{1,0:T(4,128)} %src_hbm.1, f32[1,256]{1,0:T(1,128)} %bitcast.6, f32[3,32768]{1,0:T(4,128)} %tgt_hbm.1, f32[1,32768]{1,0:T(1,128)} %bitcast.5), custom_call_target="tpu_custom_call" | custom-call | tf_op jit(solution)/shard_map/pallas_call | solution.py:332
  24.8 15.8 %all_to_all.25.first_ref = f32[32,4,128]{2,1,0:T(4,128)S(1)} all-to-all(f32[32,4,128]{2,1,0:T(4,128)S(1)} %get-tuple-element.17), channel_id=1, replica_groups=mesh['z'=8,'x'=4,'y'=4,'c'=2] {'x','y','c'}, dimensions={0} | all-to-all | bytes 131072 | tf_op jit(solution)/shard_map/all_to_all | solution.py:345
  40.6 15.7 %shard_map.60 = (f32[1024,4096]{1,0:T(8,128)S(1)}, f32[1024,4096]{1,0:T(8,128)S(1)}, f32[8,8,1024]{2,1,0:T(8,128)S(1)}, f32[8,1024]{1,0:T(8,128)S(1)}, f32[8,1024]{1,0:T(8,128)S(1)}) custom-call(f32[32,4,128]{2,1,0:T(4,128)S(1)} %all_to_all.25.first_ref, bf16[48,32768]{1,0:T(8,128)(2,1)S(1)} %get-tuple-element.18.w_ref), custom_call_target="tpu_custom_call" | custom-call | tf_op jit(solution)/shard_map/pallas_call | solution.py:332
  56.3 19.0 %all_to_all.26.cols_ref = f32[8,8,1024]{2,1,0:T(8,128)S(1)} all-to-all(f32[8,8,1024]{2,1,0:T(8,128)S(1)} %get-tuple-element.19), channel_id=1, replica_groups=mesh['z'=8,'x'=4,'y'=4,'c'=2] {'z'}, dimensions={0} | all-to-all | bytes 524288 | tf_op jit(solution)/shard_map/all_to_all | solution.py:345
  75.3 2.5 %shard_map.61 = (f32[32,8,128]{2,1,0:T(8,128)S(1)}, f32[8,1024]{1,0:T(8,128)S(1)}, f32[8,1024]{1,0:T(8,128)S(1)}) custom-call(f32[8,8,1024]{2,1,0:T(8,128)S(1)} %all_to_all.26.cols_ref, f32[1024,4096]{1,0:T(8,128)S(1)} %get-tuple-element.20.qa_ref, f32[1024,4096]{1,0:T(8,128)S(1)} %get-tuple-element.21.qb_ref, f32[8,1024]{1,0:T(8,128)S(1)} %get-tuple-element.22.shift_ref, ...), custom_call_target="tpu_custom_call" | custom-call | tf_op jit(solution)/shard_map/pallas_call | solution.py:332
  77.8 12.5 %all_to_all.27.ratio_ref = f32[32,8,128]{2,1,0:T(8,128)S(1)} all-to-all(f32[32,8,128]{2,1,0:T(8,128)S(1)} %get-tuple-element.24), channel_id=1, replica_groups=mesh['z'=8,'x'=4,'y'=4,'c'=2] {'x','y','c'}, dimensions={0} | all-to-all | bytes 262144 | tf_op jit(solution)/shard_map/all_to_all | solution.py:345
  90.4 2.6 %shard_map.62 = (f32[8,1,8320]{2,1,0:T(1,128)S(1)}, f32[1,256]{1,0:T(1,128)S(1)}) custom-call(f32[32,8,128]{2,1,0:T(8,128)S(1)} %all_to_all.27.ratio_ref, f32[1024,4096]{1,0:T(8,128)S(1)} %get-tuple-element.20.qa_ref, f32[1024,4096]{1,0:T(8,128)S(1)} %get-tuple-element.21.qb_ref, f32[8,1024]{1,0:T(8,128)S(1)} %get-tuple-element.25.src_ref, ...), custom_call_target="tpu_custom_call" | custom-call | tf_op jit(solution)/shard_map/pallas_call | solution.py:332
  93.0 14.8 %all_to_all.28.cols_ref = f32[8,1,8320]{2,1,0:T(1,128)S(1)} all-to-all(f32[8,1,8320]{2,1,0:T(1,128)S(1)} %get-tuple-element.27), channel_id=1, replica_groups=mesh['z'=8,'x'=4,'y'=4,'c'=2] {'z'}, dimensions={0} | all-to-all | bytes 532480 | tf_op jit(solution)/shard_map/all_to_all | solution.py:345
  107.8 0.7 shard_map.63
  108.5 7.2 %all_to_all.29 = f32[4,64,128]{2,1,0:T(8,128)S(1)} all-to-all(f32[4,64,128]{2,1,0:T(8,128)S(1)} %get-tuple-element.31), channel_id=1, replica_groups=mesh['z'=8,'x'=4,'y'=4,'c'=2] {'x'}, dimensions={0} | all-to-all | bytes 262144 | tf_op jit(solution)/shard_map/all_to_all | solution.py:345
  115.8 0.7 copy.7
